TPU v7x, 512 devices: a whole 4x4x16 slice. The times are simulated.
512 devices in a mesh: ma: 16 (over z_lo, y), an: 8 (over x, core), ka: 4 (over z_hi).
Axes of the slice: x: 4, y: 4, z: 16 (z_hi: 4, z_lo: 4; z = z_hi * 4 + z_lo), core: 2. Of those that a mesh axis runs over, the one named last changes fastest.
Arguments:
- left_matrix: bfloat16 [16384, 4, 1664], P(('ma', 'an'), 'ka'), may hold values from -6 to 6
- right_matrix: bfloat16 [4, 1664, 16384], P('ka', 'ma', 'an'), may hold values from -0.078125 to 0.078125
Outputs:
- product: float32 [16384, 16384], P(('ma', 'ka'), 'an')
All inputs are finite; a program needn't handle non-finite values.
Results may differ from a plain program's by a relative error of at most 0.012.
Values may be sent and summed in bfloat16 or wider, within the bound.
A program may use at most 64 MiB of HBM per device.

v0:
```python
import jax
import jax.numpy as jnp
from jax import lax
from jax.sharding import PartitionSpec as P


def per_device(left_matrix, right_matrix):
    depth_total = left_matrix.shape[2]
    column_total = right_matrix.shape[2]
    depth_rows = lax.all_gather(right_matrix, "ma", axis=1, tiled=True).reshape(
        depth_total, column_total
    )
    gathered = lax.all_gather(left_matrix, "an", axis=0, tiled=True)
    row_total = gathered.shape[0]
    left_rows = gathered.reshape(row_total, depth_total)
    partial_rows = jnp.dot(left_rows, depth_rows, preferred_element_type=jnp.float32)
    return lax.psum_scatter(
        partial_rows.astype(jnp.bfloat16).astype(jnp.float32).astype(jnp.bfloat16),
        "ka",
        scatter_dimension=0,
        tiled=True,
    ).astype(jnp.float32)


def solution(mesh):
    in_specs = (P(("ma", "an"), "ka", None), P("ka", "ma", "an"))
    out_specs = P(("ma", "ka"), "an")
    return jax.shard_map(
        per_device, mesh=mesh, in_specs=in_specs, out_specs=out_specs, check_vma=False
    )
```

profile of v0, /device:TPU:6, one launch (start us, length us, event | category | flops | bytes accessed | tf_op | source)
XLA Modules:
  0.0 333.4 jit_solution(8589654018921591415)
XLA Ops:
  6.5 0.0 all-gather.3.cloned.1.call-start
  6.5 0.7 all-gather.3.cloned.1.call-update
  7.3 0.0 all-gather.5.cloned.1.call-start
  7.3 0.7 all-gather.5.cloned.1.call-update
  8.0 0.0 reduce-scatter.2.cloned.1.call-start
  8.1 41.0 %all-gather.3.cloned.1.call-done = bf16[1024,1,1664]{2,0,1:T(8,128)(2,1)} async-done(((bf16[128,1,1664]{2,0,1:T(8,128)(2,1)}), bf16[1024,1,1664]{2,0,1:T(8,128)(2,1)}) %all-gather.3.cloned.1.call-update) | async-done | bytes 3407888 | tf_op jit(solution)/shard_map/all_gather | solution.py:13
  49.0 103.2 %all-gather.5.cloned.1.call-done = bf16[1,1664,2048]{2,1,0:T(8,128)(2,1)} async-done(((bf16[1,104,2048]{2,1,0:T(8,128)(2,1)}), bf16[1,1664,2048]{2,1,0:T(8,128)(2,1)}) %all-gather.5.cloned.1.call-update) | async-done | bytes 6815760 | tf_op jit(solution)/shard_map/all_gather | solution.py:10
  152.2 12.3 %fusion.2 = bf16[1024,2048]{1,0:T(8,128)(2,1)} fusion(bf16[1,1664,2048]{2,1,0:T(8,128)(2,1)} %all-gather.5.cloned.1.call-done, bf16[1024,1,1664]{2,0,1:T(8,128)(2,1)} %all-gather.3.cloned.1.call-done), kind=kOutput, calls=%fused_computation.2 | convolution fusion | flops 6981419008 | bytes 14417920 | tf_op jit(solution)/shard_map/dot_general | solution.py:16
  164.5 0.0 reduce-scatter.2.cloned.1.call-update
  164.5 159.6 %reduce-scatter.2.cloned.1.call-done = bf16[256,2048]{1,0:T(8,128)(2,1)} async-done(((bf16[1024,2048]{1,0:T(8,128)(2,1)}), bf16[256,2048]{1,0:T(8,128)(2,1)}) %reduce-scatter.2.cloned.1.call-update) | async-done | bytes 1048592 | tf_op jit(solution)/shard_map/reduce_scatter | solution.py:17
  324.1 2.8 convert_element_type.9
Async XLA Ops:
  6.5 42.5 %all-gather.3.cloned.1.call-start = ((), (), s32[]{:S(2)}) async-start(), calls=%async_computation.1 | async-start | bytes 3833856 | tf_op jit(solution)/shard_map/all_gather | solution.py:13
  7.3 144.9 %all-gather.5.cloned.1.call-start = ((), (), s32[]{:S(2)}) async-start(), calls=%async_computation.2 | async-start | bytes 7241728 | tf_op jit(solution)/shard_map/all_gather | solution.py:10
  8.0 316.1 %reduce-scatter.2.cloned.1.call-start = ((), (), s32[]{:S(2)}) async-start(), calls=%async_computation.3 | async-start | bytes 5242880 | tf_op jit(solution)/shard_map/reduce_scatter | solution.py:17
Sparse Core Ops, SparseCore 0:
  9.5 39.4 all-gather.2
  51.1 101.0 all-gather.4
  164.6 159.4 reduce-scatter.1
where the time goes:
time: 335 us; the launch traced here: 333 us
  waiting for transfers between devices  305 us (91%)
  between operations  13.1 us (4%)
  matrix products  12.3 us (4%)
    reduce_scatter x1, waiting for transfers between devices, per_device(): lax.psum_scatter(partial_rows.astype(jnp.bfloat16).astype(jnp.float32).as...  160 us
    all_gather x1, waiting for transfers between devices, per_device(): lax.all_gather(right_matrix, 'ma', axis=1, tiled=True)  103 us
    all_gather x1, waiting for transfers between devices, per_device(): gathered = lax.all_gather(left_matrix, 'an', axis=0, tiled=True)  41 us
    dot_general x1, matrix products, per_device(): jnp.dot(left_rows, depth_rows, preferred_element_type=jnp.float32)  12.3 us
  transfers between devices with their start and end apart: 3, of which 3 were waited for; matrix products, arithmetic and copies ran while one was open for 0% of the time, Pallas kernels for 0%

commit v1 on v0

v1 whole, which is shorter than its diff:
```python
import jax
import jax.numpy as jnp
from jax import lax
from jax.experimental import pallas as pl
from jax.experimental.pallas import tpu as pltpu
from jax.sharding import PartitionSpec as P

MESH = pl.DeviceIdType.MESH
CHUNKS, WIDTH = 2, 256


def kernel(left, right, out, hop, rows, stage, cols, total, give, take, local,
           xs_s, xs_r, zm_s, zm_r, p1_s, p1_r, p2_s, p2_r, co_s, co_r, ra_s, ra_r, ri_s, ri_r, ou_s, ou_r):
    ma, an, hi = lax.axis_index("ma"), lax.axis_index("an"), lax.axis_index("ka")
    lo, y = ma // 4, lax.rem(ma, 4)
    x, c = an // 2, lax.rem(an, 2)
    z = hi * 4 + lo

    def turn(i, d, n=4):
        return lax.rem(i + d + n, n)

    def to_x(d):
        return {"an": turn(x, d) * 2 + c}

    def to_y(d):
        return {"ma": lo * 4 + turn(y, d)}

    def to_z(d):
        level = turn(z, d, 16)
        return {"ma": lax.rem(level, 4) * 4 + y, "ka": level // 4}

    def to_hi(d):
        return {"ka": turn(hi, d)}

    to_core = {"an": x * 2 + 1 - c}

    def remote(src, dst, send, recv, device):
        return pltpu.make_async_remote_copy(
            src_ref=src, dst_ref=dst, send_sem=send, recv_sem=recv, device_id=device, device_id_type=MESH
        )

    barrier = pltpu.get_barrier_semaphore()
    friends = [to(d) for to in (to_x, to_y, to_hi) for d in (1, 2, 3)] + [to_z(1), to_z(-1), to_core]
    for friend in friends:
        pl.semaphore_signal(barrier, inc=1, device_id=friend, device_id_type=MESH)
    pl.semaphore_wait(barrier, len(friends))

    sent = []

    def send(*args):
        copy = remote(*args)
        copy.start()
        sent.append(copy)

    def await_into(dst, sem):
        remote(dst, dst, sem, sem, to_core).wait_recv()

    for d in (2, 1, 3):
        send(left.at[:, turn(x, d)], hop.at[x], xs_s.at[d - 1], xs_r.at[d - 1], to_x(d))
    own_hop = pltpu.make_async_copy(left.at[:, x], hop.at[x], local.at[0])
    own_hop.start()
    own_stage = []
    for ch in range(CHUNKS):
        for d in (2, 1, 3):
            at = pl.ds(pl.multiple_of(turn(y, d) * (CHUNKS * WIDTH) + ch * WIDTH, WIDTH), WIDTH)
            i = ch * 3 + d - 1
            send(right.at[:, at], stage.at[ch, y], ra_s.at[i], ra_r.at[i], to_y(d))
        at = pl.ds(pl.multiple_of(y * (CHUNKS * WIDTH) + ch * WIDTH, WIDTH), WIDTH)
        own_stage.append(pltpu.make_async_copy(right.at[:, at], stage.at[ch, y], local.at[1 + ch]))
        own_stage[-1].start()

    own_hop.wait()
    for d in (1, 2, 3):
        await_into(hop.at[turn(x, -d)], xs_r.at[d - 1])
    for d in (2, 1, 3):
        send(hop.at[turn(hi, d)], rows.at[hi, y, c, :, x], zm_s.at[d - 1], zm_r.at[d - 1], to_hi(d))
    own_rows = pltpu.make_async_copy(hop.at[hi], rows.at[hi, y, c, :, x], local.at[3])
    own_rows.start()

    def settle(ch):
        own_stage[ch].wait()
        for d in (1, 2, 3):
            await_into(stage.at[ch, turn(y, -d)], ra_r.at[ch * 3 + d - 1])
        block = stage[ch].astype(jnp.float32).reshape(cols.shape[2] * cols.shape[3], WIDTH)
        cols[ch, z] = block.astype(jnp.bfloat16).reshape(cols.shape[2:])

    def ring_index(ch, s, way, sub):
        return ((ch * 8 + s - 1) * 2 + way) * 2 + sub

    def ring(ch, s):
        for sub in (0, 1):
            for way, sign in ((0, 1), (1, -1)):
                block = cols.at[ch, turn(z, -sign * (s - 1), 16), sub]
                if s > 1:
                    await_into(block, ri_r.at[ring_index(ch, s - 1, way, sub)])
                if s == 8 and sub != way:
                    continue
                i = ring_index(ch, s, way, sub)
                send(block, block, ri_s.at[i], ri_r.at[i], to_z(sign))

    def ring_end(ch):
        for way in (0, 1):
            await_into(cols.at[ch, turn(z, 8, 16), way], ri_r.at[ring_index(ch, 8, way, way)])

    def gather_one():
        own_rows.wait()
        for d in (1, 2, 3):
            await_into(rows.at[turn(hi, -d), y, c, :, x], zm_r.at[d - 1])
        for d in (2, 1, 3):
            mine = rows.at[:, y, c, 0, x]
            send(mine, mine, p1_s.at[d - 1], p1_r.at[d - 1], to_x(d))
            mine = rows.at[:, y, c, 1, x]
            send(mine, mine, p1_s.at[d + 2], p1_r.at[d + 2], to_y(d))

    def gather_two():
        for d in (1, 2, 3):
            await_into(rows.at[:, y, c, 0, turn(x, -d)], p1_r.at[d - 1])
            await_into(rows.at[:, turn(y, -d), c, 1, x], p1_r.at[d + 2])
        for k in range(4):
            for d in (2, 1, 3):
                i = (k * 3 + d - 1) * 2
                mine = rows.at[turn(hi, k), y, c, 0]
                send(mine, mine, p2_s.at[i], p2_r.at[i], to_y(d))
                mine = rows.at[turn(hi, k), :, c, 1, x]
                send(mine, mine, p2_s.at[i + 1], p2_r.at[i + 1], to_x(d))
        mine = rows.at[:, y, c, 0]
        send(mine, mine, co_s.at[24], co_r.at[24], to_core)
        mine = rows.at[:, :, c, 1, x]
        send(mine, mine, co_s.at[25], co_r.at[25], to_core)

    def pass_on(k):
        for d in (1, 3, 2):
            i = (k * 3 + d - 1) * 2
            got = rows.at[turn(hi, k), turn(y, -d), c, 0]
            await_into(got, p2_r.at[i])
            send(got, got, co_s.at[i], co_r.at[i], to_core)
            got = rows.at[turn(hi, k), :, c, 1, turn(x, -d)]
            await_into(got, p2_r.at[i + 1])
            send(got, got, co_s.at[i + 1], co_r.at[i + 1], to_core)

    def get_rest(k):
        if k == 0:
            await_into(rows.at[:, y, 1 - c, 0], co_r.at[24])
            await_into(rows.at[:, :, 1 - c, 1, x], co_r.at[25])
        for d in (1, 3, 2):
            i = (k * 3 + d - 1) * 2
            await_into(rows.at[turn(hi, k), turn(y, -d), 1 - c, 0], co_r.at[i])
            await_into(rows.at[turn(hi, k), :, 1 - c, 1, turn(x, -d)], co_r.at[i + 1])

    def multiply(ch, k, first=False):
        block = turn(hi, k)

        def one(i, carry):
            a = rows[block, i].reshape(256, rows.shape[-1])
            b = cols[ch, pl.ds(block * 4, 4)].reshape(rows.shape[-1], WIDTH)
            term = jnp.dot(a, b, preferred_element_type=jnp.float32)
            total[ch, i] = term if first else total[ch, i] + term
            return carry

        lax.fori_loop(0, 4, one, 0)

    def hand_out(ch):
        give[ch] = total[ch].astype(jnp.bfloat16)
        for d in (2, 1, 3):
            i = ch * 3 + d - 1
            send(give.at[ch, turn(y, d)], take.at[ch, y], ou_s.at[i], ou_r.at[i], to_y(d))
        own = pltpu.make_async_copy(give.at[ch, y], take.at[ch, y], local.at[4 + ch])
        own.start()
        return own

    def collect(ch, own):
        own.wait()
        for d in (1, 2, 3):
            await_into(take.at[ch, turn(y, -d)], ou_r.at[ch * 3 + d - 1])
        for i in range(4):
            out[:, pl.ds((i * CHUNKS + ch) * WIDTH, WIDTH)] = take[ch, i]

    settle(0)
    ring(0, 1)
    settle(1)
    ring(0, 2)
    ring(0, 3)
    gather_one()
    ring(0, 4)
    ring(0, 5)
    ring(0, 6)
    gather_two()
    ring(0, 7)
    ring(0, 8)
    ring(1, 1)
    ring(1, 2)
    pass_on(0)
    ring(1, 3)
    pass_on(1)
    ring(1, 4)
    pass_on(2)
    ring(1, 5)
    pass_on(3)
    ring(1, 6)
    ring_end(0)
    get_rest(0)
    multiply(0, 0, first=True)
    get_rest(1)
    multiply(0, 1)
    ring(1, 7)
    get_rest(2)
    multiply(0, 2)
    get_rest(3)
    multiply(0, 3)
    ring(1, 8)
    own0 = hand_out(0)
    for k in (0, 1, 3):
        multiply(1, k, first=k == 0)
    collect(0, own0)
    ring_end(1)
    multiply(1, 2)
    own1 = hand_out(1)
    collect(1, own1)
    for copy in sent:
        copy.wait_send()


def per_device(left_matrix, right_matrix):
    depth = left_matrix.shape[2]
    left = left_matrix.reshape(2, 4, 16, depth)
    right = right_matrix.reshape(right_matrix.shape[1:])
    dma = pltpu.SemaphoreType.DMA
    counts = (3, 3, 6, 24, 26, 6, CHUNKS * 32, 6)
    product = pl.pallas_call(
        kernel,
        out_shape=jax.ShapeDtypeStruct((256, right.shape[1]), jnp.bfloat16),
        in_specs=[pl.BlockSpec(memory_space=pl.ANY)] * 2,
        out_specs=pl.BlockSpec(memory_space=pltpu.VMEM),
        scratch_shapes=[
            pltpu.VMEM((4, 2, 16, depth), jnp.bfloat16),
            pltpu.VMEM((4, 4, 2, 2, 4, 16, depth), jnp.bfloat16),
            pltpu.VMEM((CHUNKS, 4, right.shape[0], WIDTH), jnp.bfloat16),
            pltpu.VMEM((CHUNKS, 16, 2, right.shape[0] * 2, WIDTH), jnp.bfloat16),
            pltpu.VMEM((CHUNKS, 4, 256, WIDTH), jnp.float32),
            pltpu.VMEM((CHUNKS, 4, 256, WIDTH), jnp.bfloat16),
            pltpu.VMEM((CHUNKS, 4, 256, WIDTH), jnp.bfloat16),
            dma((6,)),
        ]
        + [dma((n,)) for n in counts for _ in range(2)],
        compiler_params=pltpu.CompilerParams(
            collective_id=0, has_side_effects=True, vmem_limit_bytes=56 * 2**20
        ),
    )(left, right)
    return product.astype(jnp.float32)


def solution(mesh):
    in_specs = (P(("ma", "an"), "ka", None), P("ka", "ma", "an"))
    out_specs = P(("ma", "ka"), "an")
    return jax.shard_map(per_device, mesh=mesh, in_specs=in_specs, out_specs=out_specs, check_vma=False)
```

time: 335 us -> 136 us (0.41)
  waiting for transfers between devices: 305 us -> 0 us
  Pallas kernels: 0 us -> 131 us
  between operations: 13.1 us -> 0.01 us
  matrix products: 12.3 us -> 0 us
    reduce_scatter x1 -> x0, waiting for transfers between devices: 160 us -> none  [per_device(): lax.psum_scatter(partial_rows.astype(jnp.bfloat16).astype(jnp.float32).as...]
    all_gather x2 -> x0, waiting for transfers between devices: 144 us -> none  [the longest x1 103 us: per_device(): lax.all_gather(right_matrix, 'ma', axis=1, tiled=True)]
    pallas_call x0 -> x1, Pallas kernels: none -> 131 us  [per_device(): pl.pallas_call(kernel, out_shape=jax.ShapeDtypeStruct((256, right.shape[1...]
    dot_general x1 -> x0, matrix products: 12.3 us -> none  [per_device(): jnp.dot(left_rows, depth_rows, preferred_element_type=jnp.float32)]
  transfers between devices with their start and end apart: 3 -> 0, of which waited for: 3 -> 0; matrix products, arithmetic and copies ran while one was open for 0% -> 0% of each run, Pallas kernels for 0% -> 0%
where the time goes in v1:
time: 136 us; the launch traced here: 134 us
  Pallas kernels  131 us (96%)
  other arithmetic  2.79 us (2%)
    pallas_call x1, Pallas kernels, per_device(): pl.pallas_call(kernel, out_shape=jax.ShapeDtypeStruct((256, right.shape[1...  131 us
    convert_element_type x1, other arithmetic, per_device(): return product.astype(jnp.float32)  2.79 us

profile of v1, /device:TPU:6, one launch (start us, length us, event | category | flops | bytes accessed | tf_op | source)
XLA Modules:
  0.0 134.1 jit_solution(1037892861738722428)
XLA Ops:
  0.0 131.3 %shard_map.28 = bf16[256,2048]{1,0:T(8,128)(2,1)} custom-call(bf16[2,4,16,1664]{3,2,1,0:T(8,128)(2,1)} %bitcast.2, bf16[104,2048]{1,0:T(8,128)(2,1)} %bitcast.3), custom_call_target="tpu_custom_call" | custom-call | tf_op jit(solution)/shard_map/pallas_call | solution.py:229
  131.3 2.8 %convert_element_type.3 = f32[256,2048]{1,0:T(8,128)} convert(bf16[256,2048]{1,0:T(8,128)(2,1)} %shard_map.28) | non-fusion elementwise | flops 524288 | bytes 3145728 | tf_op jit(solution)/shard_map/convert_element_type | solution.py:249

commit v2 on v0

v2 whole, which is shorter than its diff:
```python
import jax
import jax.numpy as jnp
from jax import lax
from jax.experimental import pallas as pl
from jax.experimental.pallas import tpu as pltpu
from jax.sharding import PartitionSpec as P

MESH = pl.DeviceIdType.MESH
WIDTHS = (256, 256)
STARTS = tuple(sum(WIDTHS[:ch]) for ch in range(len(WIDTHS)))
QUARTER = sum(WIDTHS)
CHUNKS = len(WIDTHS)


def kernel(left, right, out, hop, relay, rows, *refs):
    refs = list(refs)

    def take_refs(n):
        taken, refs[:n] = refs[:n], []
        return taken

    stage, cols, total, give, take = (take_refs(CHUNKS) for _ in range(5))
    up, down, local, xs_s, xs_r, zm_s, zm_r, p1_s, p1_r, p2_s, p2_r, co_s, co_r, ra_s, ra_r, ri_s, ri_r, ou_s, ou_r = refs
    depth = rows.shape[-1]
    ma, an, hi = lax.axis_index("ma"), lax.axis_index("an"), lax.axis_index("ka")
    lo, y = ma // 4, lax.rem(ma, 4)
    x, c = an // 2, lax.rem(an, 2)
    z = hi * 4 + lo

    def turn(i, d, n=4):
        return lax.rem(i + d + n, n)

    def to_x(d):
        return {"an": turn(x, d) * 2 + c}

    def to_y(d):
        return {"ma": lo * 4 + turn(y, d)}

    def to_z(d):
        level = turn(z, d, 16)
        return {"ma": lax.rem(level, 4) * 4 + y, "ka": level // 4}

    def to_hi(d):
        return {"ka": turn(hi, d)}

    to_core = {"an": x * 2 + 1 - c}

    def remote(src, dst, send, recv, device):
        return pltpu.make_async_remote_copy(
            src_ref=src, dst_ref=dst, send_sem=send, recv_sem=recv, device_id=device, device_id_type=MESH
        )

    barrier = pltpu.get_barrier_semaphore()
    friends = [to(d) for to in (to_x, to_y) for d in (1, 2, 3)] + [to_z(-1), to_core]
    for friend in friends:
        pl.semaphore_signal(barrier, inc=1, device_id=friend, device_id_type=MESH)
    pl.semaphore_wait(barrier, len(friends))

    sent = []

    def send(*args):
        copy = remote(*args)
        copy.start()
        sent.append(copy)

    def await_into(dst, sem):
        remote(dst, dst, sem, sem, to_core).wait_recv()

    def hear(r):
        if r >= 2:
            pl.semaphore_wait(down.at[r - 1], 1)
        if r >= 3:
            pl.semaphore_wait(up.at[r - 1], 1)
        if r <= 4:
            pl.semaphore_signal(down.at[r], inc=1, device_id=to_z(1), device_id_type=MESH)
        if 2 <= r <= 4:
            pl.semaphore_signal(up.at[r], inc=1, device_id=to_z(-1), device_id_type=MESH)

    own = {}

    def start_local(src, dst, i):
        own[i] = pltpu.make_async_copy(src, dst, local.at[i])
        own[i].start()

    def columns(ch, of):
        return pl.ds(pl.multiple_of(of * QUARTER + STARTS[ch], 128), WIDTHS[ch])

    def scatter():
        for d in (2, 1, 3):
            send(left.at[:, turn(x, d)], hop.at[x], xs_s.at[d - 1], xs_r.at[d - 1], to_x(d))
        start_local(left.at[:, x], hop.at[x], 0)

    def spread(ch):
        for d in (2, 1, 3):
            i = ch * 3 + d - 1
            send(right.at[:, columns(ch, turn(y, d))], stage[ch].at[y], ra_s.at[i], ra_r.at[i], to_y(d))
        start_local(right.at[:, columns(ch, y)], stage[ch].at[y], 2 + ch)

    def settle(ch):
        own[2 + ch].wait()
        for d in (1, 2, 3):
            await_into(stage[ch].at[turn(y, -d)], ra_r.at[ch * 3 + d - 1])
        block = stage[ch][...].astype(jnp.float32).reshape(-1, WIDTHS[ch])
        cols[ch][z] = block.astype(jnp.bfloat16).reshape(cols[ch].shape[1:])

    def scattered():
        own[0].wait()
        for d in (1, 2, 3):
            await_into(hop.at[turn(x, -d)], xs_r.at[d - 1])
        start_local(hop.at[hi], rows.at[hi, y, c, :, x], 1)

    def lift(d):
        if d == 2:
            for half, way in ((0, 1), (1, 3)):
                send(hop.at[turn(hi, 2), half], relay.at[half], zm_s.at[half], zm_r.at[half], to_hi(way))
        else:
            send(hop.at[turn(hi, d)], rows.at[hi, y, c, :, x], zm_s.at[1 + d], zm_r.at[1 + d], to_hi(d))

    def lift_on():
        for half, way in ((0, 1), (1, 3)):
            await_into(relay.at[half], zm_r.at[half])
            i = 3 + 2 * half
            send(relay.at[half], rows.at[turn(hi, -way), y, c, half, x], zm_s.at[i], zm_r.at[i], to_hi(way))

    def ring_index(ch, s, way, sub):
        return ((ch * 8 + s - 1) * 2 + way) * 2 + sub

    def ring(ch, s, ways=(0, 1)):
        for sub in (0, 1):
            for way in ways:
                sign = 1 - 2 * way
                block = cols[ch].at[turn(z, -sign * (s - 1), 16), sub]
                if s > 1:
                    await_into(block, ri_r.at[ring_index(ch, s - 1, way, sub)])
                if s == 8 and sub != way:
                    continue
                i = ring_index(ch, s, way, sub)
                send(block, block, ri_s.at[i], ri_r.at[i], to_z(sign))

    def ring_end(ch):
        for way in (0, 1):
            await_into(cols[ch].at[turn(z, 8, 16), way], ri_r.at[ring_index(ch, 8, way, way)])

    def gather_one(k):
        block = turn(hi, k)
        if k == 0:
            own[1].wait()
        else:
            if k == 2:
                for half in (0, 1):
                    await_into(rows.at[block, y, c, half, x], zm_r.at[3 + 2 * half])
            else:
                await_into(rows.at[block, y, c, :, x], zm_r.at[5 - k])
        for d in (2, 1, 3):
            i = (k * 3 + d - 1) * 2
            for half, to in ((0, to_x(d)), (1, to_y(d))):
                mine = rows.at[block, y, c, half, x]
                send(mine, mine, p1_s.at[i + half], p1_r.at[i + half], to)

    def gather_two(k):
        block = turn(hi, k)
        for d in (1, 3, 2):
            i = (k * 3 + d - 1) * 2
            await_into(rows.at[block, y, c, 0, turn(x, -d)], p1_r.at[i])
            await_into(rows.at[block, turn(y, -d), c, 1, x], p1_r.at[i + 1])
        for d in (2, 1, 3, 0):
            for half, mine in ((0, rows.at[block, y, c, 0]), (1, rows.at[block, :, c, 1, x])):
                if d == 0:
                    i = k * 8 + half
                    send(mine, mine, co_s.at[i], co_r.at[i], to_core)
                else:
                    i = (k * 3 + d - 1) * 2 + half
                    send(mine, mine, p2_s.at[i], p2_r.at[i], to_x(d) if half else to_y(d))

    def pass_on(k):
        block = turn(hi, k)
        for d in (1, 3, 2):
            i, j = (k * 3 + d - 1) * 2, k * 8 + 2 * d
            for half, got in ((0, rows.at[block, turn(y, -d), c, 0]), (1, rows.at[block, :, c, 1, turn(x, -d)])):
                await_into(got, p2_r.at[i + half])
                send(got, got, co_s.at[j + half], co_r.at[j + half], to_core)

    def get_rest(k):
        block = turn(hi, k)
        for d in (0, 1, 3, 2):
            j = k * 8 + 2 * d
            await_into(rows.at[block, turn(y, -d), 1 - c, 0], co_r.at[j])
            await_into(rows.at[block, :, 1 - c, 1, turn(x, -d)], co_r.at[j + 1])

    begun = set()

    def multiply(ch, k):
        block, first = turn(hi, k), ch not in begun
        begun.add(ch)

        a = rows[block].reshape(-1, depth)
        b = cols[ch][pl.ds(block * 4, 4)].reshape(depth, WIDTHS[ch])
        term = jnp.dot(a, b, preferred_element_type=jnp.float32)
        total[ch][...] = term if first else total[ch][...] + term

    def hand_out(ch, k):
        block = turn(hi, k)
        for d in (2, 1, 3, 0):
            of = turn(y, d)
            at = pl.ds(pl.multiple_of(of * 256, 256), 256)
            a = rows[block, of].reshape(256, depth)
            b = cols[ch][pl.ds(block * 4, 4)].reshape(depth, WIDTHS[ch])
            term = jnp.dot(a, b, preferred_element_type=jnp.float32)
            give[ch][of] = (total[ch][at] + term).astype(jnp.bfloat16)
            if d:
                i = ch * 3 + d - 1
                send(give[ch].at[of], take[ch].at[y], ou_s.at[i], ou_r.at[i], to_y(d))
        start_local(give[ch].at[y], take[ch].at[y], 2 + CHUNKS + ch)

    def collect(ch):
        own[2 + CHUNKS + ch].wait()
        for d in (1, 2, 3):
            await_into(take[ch].at[turn(y, -d)], ou_r.at[ch * 3 + d - 1])
        for i in range(4):
            out[:, pl.ds(i * QUARTER + STARTS[ch], WIDTHS[ch])] = take[ch][i]

    hear(1)
    spread(0)
    scatter()
    spread(1)
    settle(0)
    ring(0, 1, (0,))
    hear(2)
    ring(0, 1, (1,))
    settle(1)
    scattered()
    gather_one(0)
    hear(3)
    hear(4)
    hear(5)
    lift(1)
    lift(3)
    lift(2)
    ring(0, 2)
    gather_two(0)
    ring(0, 3)
    ring(0, 4)
    lift_on()
    ring(1, 1)
    gather_one(1)
    gather_one(3)
    pass_on(0)
    ring(0, 5)
    gather_two(1)
    gather_two(3)
    ring(1, 2)
    gather_one(2)
    ring(0, 6)
    get_rest(0)
    ring(1, 3)
    multiply(0, 0)
    gather_two(2)
    pass_on(1)
    pass_on(3)
    ring(0, 7)
    get_rest(1)
    get_rest(3)
    ring(1, 4)
    ring(0, 8)
    pass_on(2)
    multiply(0, 1)
    multiply(0, 3)
    get_rest(2)
    ring(1, 5)
    ring_end(0)
    hand_out(0, 2)
    ring(1, 6)
    multiply(1, 0)
    ring(1, 7)
    collect(0)
    ring(1, 8)
    multiply(1, 1)
    multiply(1, 3)
    ring_end(1)
    hand_out(1, 2)
    collect(1)
    for copy in sent:
        copy.wait_send()


def per_device(left_matrix, right_matrix):
    depth, strip = left_matrix.shape[2], right_matrix.shape[1]
    left = left_matrix.reshape(2, 4, 16, depth)
    right = right_matrix.reshape(right_matrix.shape[1:])
    dma, regular = pltpu.SemaphoreType.DMA, pltpu.SemaphoreType.REGULAR
    counts = (3, 6, 24, 24, 32, CHUNKS * 3, CHUNKS * 32, CHUNKS * 3)
    bf16 = jnp.bfloat16
    product = pl.pallas_call(
        kernel,
        out_shape=pltpu.VMEM((256, right.shape[1]), bf16),
        in_specs=[pl.BlockSpec(memory_space=pl.ANY)] * 2,
        out_specs=pl.BlockSpec(memory_space=pltpu.VMEM),
        scratch_shapes=[
            pltpu.VMEM((4, 2, 16, depth), bf16),
            pltpu.VMEM((2, 16, depth), bf16),
            pltpu.VMEM((4, 4, 2, 2, 4, 16, depth), bf16),
            *[pltpu.VMEM((4, strip, width), bf16) for width in WIDTHS],
            *[pltpu.VMEM((16, 2, strip * 2, width), bf16) for width in WIDTHS],
            *[pltpu.VMEM((1024, width), jnp.float32) for width in WIDTHS],
            *[pltpu.VMEM((4, 256, width), bf16) for width in WIDTHS * 2],
            regular((5,)),
            regular((5,)),
            dma((2 + 2 * CHUNKS,)),
            *[dma((n,)) for n in counts for _ in range(2)],
        ],
        compiler_params=pltpu.CompilerParams(
            collective_id=0, has_side_effects=True, vmem_limit_bytes=56 * 2**20
        ),
    )(left, right)
    return product.astype(jnp.float32)


def solution(mesh):
    in_specs = (P(("ma", "an"), "ka", None), P("ka", "ma", "an"))
    out_specs = P(("ma", "ka"), "an")
    return jax.shard_map(per_device, mesh=mesh, in_specs=in_specs, out_specs=out_specs, check_vma=False)
```

time: 335 us -> 121 us (0.36)
  waiting for transfers between devices: 305 us -> 0 us
  Pallas kernels: 0 us -> 119 us
  between operations: 13.1 us -> 0.01 us
  matrix products: 12.3 us -> 0 us
    reduce_scatter x1 -> x0, waiting for transfers between devices: 160 us -> none  [per_device(): lax.psum_scatter(partial_rows.astype(jnp.bfloat16).astype(jnp.float32).as...]
    all_gather x2 -> x0, waiting for transfers between devices: 144 us -> none  [the longest x1 103 us: per_device(): lax.all_gather(right_matrix, 'ma', axis=1, tiled=True)]
    pallas_call x0 -> x1, Pallas kernels: none -> 119 us  [per_device(): pl.pallas_call(kernel, out_shape=pltpu.VMEM((256, right.shape[1]), bf16),...]
    dot_general x1 -> x0, matrix products: 12.3 us -> none  [per_device(): jnp.dot(left_rows, depth_rows, preferred_element_type=jnp.float32)]
  transfers between devices with their start and end apart: 3 -> 0, of which waited for: 3 -> 0; matrix products, arithmetic and copies ran while one was open for 0% -> 0% of each run, Pallas kernels for 0% -> 0%
where the time goes in v2:
time: 121 us
  Pallas kernels  119 us (98%)
  other arithmetic  1.57 us (1%)
    pallas_call x1, Pallas kernels, per_device(): pl.pallas_call(kernel, out_shape=pltpu.VMEM((256, right.shape[1]), bf16),...  119 us

profile of v2, /device:TPU:6, one launch (start us, length us, event | category | flops | bytes accessed | tf_op | source)
XLA Modules:
  0.0 121.0 jit_solution(5300687488076035609)
XLA Ops:
  0.0 119.5 %shard_map.28 = bf16[256,2048]{1,0:T(8,128)(2,1)S(1)} custom-call(bf16[2,4,16,1664]{3,2,1,0:T(8,128)(2,1)} %bitcast.2, bf16[104,2048]{1,0:T(8,128)(2,1)} %bitcast.3), custom_call_target="tpu_custom_call" | custom-call | tf_op jit(solution)/shard_map/pallas_call | solution.py:293
  119.5 1.6 %convert_element_type.3 = f32[256,2048]{1,0:T(8,128)} convert(bf16[256,2048]{1,0:T(8,128)(2,1)S(1)} %shard_map.28) | non-fusion elementwise | flops 524288 | bytes 3145728 | tf_op jit(solution)/shard_map/convert_element_type | solution.py:315

commit v3 on v2

--- a/solution.py
+++ b/solution.py
@@ -62,6 +62,10 @@
         copy = remote(*args)
         copy.start()
         sent.append(copy)
+
+    def flush(keep):
+        while len(sent) > keep:
+            sent.pop(0).wait_send()
 
     def await_into(dst, sem):
         remote(dst, dst, sem, sem, to_core).wait_recv()
@@ -224,9 +228,9 @@
     scatter()
     spread(1)
     settle(0)
-    ring(0, 1, (0,))
+    ring(0, 1, ways=(0,))
     hear(2)
-    ring(0, 1, (1,))
+    ring(0, 1, ways=(1,))
     settle(1)
     scattered()
     gather_one(0)
@@ -239,38 +243,38 @@
     ring(0, 2)
     gather_two(0)
     ring(0, 3)
+    ring(1, 1)
     ring(0, 4)
+    ring(1, 2)
     lift_on()
-    ring(1, 1)
     gather_one(1)
     gather_one(3)
     pass_on(0)
     ring(0, 5)
     gather_two(1)
     gather_two(3)
-    ring(1, 2)
+    ring(1, 3)
     gather_one(2)
     ring(0, 6)
     get_rest(0)
-    ring(1, 3)
+    ring(1, 4)
     multiply(0, 0)
     gather_two(2)
+    ring(0, 7)
     pass_on(1)
     pass_on(3)
-    ring(0, 7)
+    ring(1, 5)
     get_rest(1)
     get_rest(3)
-    ring(1, 4)
     ring(0, 8)
+    multiply(1, 0)
+    multiply(0, 1)
     pass_on(2)
-    multiply(0, 1)
+    ring(1, 6)
     multiply(0, 3)
     get_rest(2)
-    ring(1, 5)
     ring_end(0)
     hand_out(0, 2)
-    ring(1, 6)
-    multiply(1, 0)
     ring(1, 7)
     collect(0)
     ring(1, 8)
@@ -278,9 +282,9 @@
     multiply(1, 3)
     ring_end(1)
     hand_out(1, 2)
+    flush(3)
     collect(1)
-    for copy in sent:
-        copy.wait_send()
+    flush(0)
 
 
 def per_device(left_matrix, right_matrix):

time: 121 us -> 119 us (0.983)
    pallas_call x1, Pallas kernels: 119 us -> 118 us  [per_device(): pl.pallas_call(kernel, out_shape=pltpu.VMEM((256, right.shape[1]), bf16),...]
where the time goes in v3:
time: 119 us
  Pallas kernels  118 us (99%)
  other arithmetic  1.57 us (1%)
    pallas_call x1, Pallas kernels, per_device(): pl.pallas_call(kernel, out_shape=pltpu.VMEM((256, right.shape[1]), bf16),...  118 us

profile of v3, /device:TPU:6, one launch (start us, length us, event | category | flops | bytes accessed | tf_op | source)
XLA Modules:
  0.0 119.2 jit_solution(14259645300577147250)
XLA Ops:
  0.0 117.6 %shard_map.28 = bf16[256,2048]{1,0:T(8,128)(2,1)S(1)} custom-call(bf16[2,4,16,1664]{3,2,1,0:T(8,128)(2,1)} %bitcast.2, bf16[104,2048]{1,0:T(8,128)(2,1)} %bitcast.3), custom_call_target="tpu_custom_call" | custom-call | tf_op jit(solution)/shard_map/pallas_call | solution.py:297
  117.6 1.6 %convert_element_type.3 = f32[256,2048]{1,0:T(8,128)} convert(bf16[256,2048]{1,0:T(8,128)(2,1)S(1)} %shard_map.28) | non-fusion elementwise | flops 524288 | bytes 3145728 | tf_op jit(solution)/shard_map/convert_element_type | solution.py:319

commit v4 on v3

--- a/solution.py
+++ b/solution.py
@@ -129,9 +129,9 @@
     def ring_index(ch, s, way, sub):
         return ((ch * 8 + s - 1) * 2 + way) * 2 + sub
 
-    def ring(ch, s, ways=(0, 1)):
+    def ring(ch, s):
         for sub in (0, 1):
-            for way in ways:
+            for way in (0, 1):
                 sign = 1 - 2 * way
                 block = cols[ch].at[turn(z, -sign * (s - 1), 16), sub]
                 if s > 1:
@@ -197,10 +197,15 @@
         block, first = turn(hi, k), ch not in begun
         begun.add(ch)
 
-        a = rows[block].reshape(-1, depth)
-        b = cols[ch][pl.ds(block * 4, 4)].reshape(depth, WIDTHS[ch])
-        term = jnp.dot(a, b, preferred_element_type=jnp.float32)
-        total[ch][...] = term if first else total[ch][...] + term
+        def half(i, carry):
+            at = pl.ds(pl.multiple_of(i * 512, 512), 512)
+            a = rows[block, pl.ds(i * 2, 2)].reshape(512, depth)
+            b = cols[ch][pl.ds(block * 4, 4)].reshape(depth, WIDTHS[ch])
+            term = jnp.dot(a, b, preferred_element_type=jnp.float32)
+            total[ch][at] = term if first else total[ch][at] + term
+            return carry
+
+        lax.fori_loop(0, 2, half, 0)
 
     def hand_out(ch, k):
         block = turn(hi, k)
@@ -226,20 +231,19 @@
     hear(1)
     spread(0)
     scatter()
+    hear(2)
+    settle(0)
+    ring(0, 1)
     spread(1)
-    settle(0)
-    ring(0, 1, ways=(0,))
-    hear(2)
-    ring(0, 1, ways=(1,))
-    settle(1)
+    hear(3)
     scattered()
+    hear(4)
     gather_one(0)
-    hear(3)
-    hear(4)
     hear(5)
     lift(1)
     lift(3)
     lift(2)
+    settle(1)
     ring(0, 2)
     gather_two(0)
     ring(0, 3)
@@ -276,9 +280,9 @@
     ring_end(0)
     hand_out(0, 2)
     ring(1, 7)
-    collect(0)
     ring(1, 8)
     multiply(1, 1)
+    collect(0)
     multiply(1, 3)
     ring_end(1)
     hand_out(1, 2)

time: 119 us -> 119 us (level); the launches traced: 119 us -> 118 us
  Pallas kernels: 118 us -> 116 us
    pallas_call x1, Pallas kernels: 118 us -> 116 us  [per_device(): pl.pallas_call(kernel, out_shape=pltpu.VMEM((256, right.shape[1]), bf16),...]
where the time goes in v4:
time: 119 us; the launch traced here: 118 us
  Pallas kernels  116 us (97%)
  other arithmetic  1.57 us (1%)
    pallas_call x1, Pallas kernels, per_device(): pl.pallas_call(kernel, out_shape=pltpu.VMEM((256, right.shape[1]), bf16),...  116 us

profile of v4, /device:TPU:6, one launch (start us, length us, event | category | flops | bytes accessed | tf_op | source)
XLA Modules:
  0.0 118.0 jit_solution(12886562576483665520)
XLA Ops:
  0.0 116.4 %shard_map.28 = bf16[256,2048]{1,0:T(8,128)(2,1)S(1)} custom-call(bf16[2,4,16,1664]{3,2,1,0:T(8,128)(2,1)} %bitcast.2, bf16[104,2048]{1,0:T(8,128)(2,1)} %bitcast.3), custom_call_target="tpu_custom_call" | custom-call | tf_op jit(solution)/shard_map/pallas_call | solution.py:301
  116.4 1.6 %convert_element_type.3 = f32[256,2048]{1,0:T(8,128)} convert(bf16[256,2048]{1,0:T(8,128)(2,1)S(1)} %shard_map.28) | non-fusion elementwise | flops 524288 | bytes 3145728 | tf_op jit(solution)/shard_map/convert_element_type | solution.py:323
